TPU v7x, 256 devices: a whole 4x4x8 slice. The times are simulated.
256 devices in a mesh: expert: 64 (over z, x, core), zero: 4 (over y).
Axes of the slice: x: 4, y: 4, z: 8, core: 2. Of those that a mesh axis runs over, the one named last changes fastest.
Arguments:
- cotangent: bfloat16 [32768, 2048], P(('expert', 'zero')), may hold values from -0.59765625 to 0.59765625
- gates: float32 [32768, 8], P(('expert', 'zero')), may hold values from 0.05 to 1
- expert_ids: int32 [32768, 8], P(('expert', 'zero')), may hold values from 0 to 127, all different within a row; in each aligned block of 128 rows (0 to 127, 128 to 255, ...) at most 16 rows name the same one
- hidden: bfloat16 [128, 4096, 768], P('expert', 'zero'), may hold values from -6 to 6
- momentum_left: float32 [128, 768, 32], P('expert', 'zero'), may hold values from -6 to 6
- momentum_right: float32 [128, 32, 2048], P('expert', None, 'zero'), may hold values from -1 to 1
- sketch: float32 [128, 2048, 32], P('expert'), may hold values from -6 to 6
Outputs:
- basis: float32 [128, 768, 32], P('expert', 'zero')
- coefficients: float32 [128, 32, 2048], P('expert', None, 'zero')
Inputs may be any that keep to these rules, and one draw needn't show every extreme that they name: `expert_ids`: among the 128 tokens of one device (an aligned block of rows) no expert is named more than 16 times, a bound that some block reaches; the 8 experts of a token differ.
All inputs are finite; a program needn't handle non-finite values.
Results may differ from a plain program's by a relative error of at most 0.0035.
Values may be sent and summed in bfloat16 or wider, within the bound.
No kernel may reach another device: no remote copies, remote signals or barrier semaphores. Data moves between devices by JAX's collectives and lax.ppermute only.
A program may use at most 128 MiB of HBM per device.

v0:
```python
import jax
import jax.numpy as jnp
from jax import lax
from jax.sharding import PartitionSpec as P

FF = 768
CAP = 16
MOMENTUM_DECAY = 0.9


def slot_table(ids_block, count):
    flat = ids_block.reshape(-1)
    onehot = (flat[:, None] == jnp.arange(count, dtype=jnp.int32)[None, :]).astype(jnp.int32)
    before = jnp.cumsum(onehot, axis=0) - onehot
    return jnp.sum(before * onehot, axis=1)


def orthonormal(rows_y):
    highest = lax.Precision.HIGHEST
    local_gram = jnp.einsum("efr,efs->ers", rows_y, rows_y, precision=highest)
    gram = lax.psum(local_gram, "zero") / FF
    lower = jnp.linalg.cholesky(gram)
    basis_t = lax.linalg.triangular_solve(
        lower, jnp.swapaxes(rows_y, 1, 2), left_side=True, lower=True
    )
    return jnp.swapaxes(basis_t, 1, 2)


def body(cotangent, gates, expert_ids, hidden, momentum_left, momentum_right, sketch):
    highest = lax.Precision.HIGHEST
    local_experts = hidden.shape[0]
    experts = local_experts * lax.axis_size("expert")
    width = cotangent.shape[1]
    slots = slot_table(expert_ids, experts)
    scaled = (gates[:, :, None] * cotangent[:, None, :].astype(jnp.float32)).astype(jnp.bfloat16)
    target = expert_ids.reshape(-1) * CAP + slots
    outgoing = (
        jnp.zeros((experts * CAP, width), jnp.bfloat16).at[target].set(scaled.reshape(-1, width))
    )
    outgoing = outgoing.reshape(experts, CAP, width)
    arrived = lax.all_to_all(outgoing, "expert", split_axis=0, concat_axis=1, tiled=True)
    right_full = lax.all_gather(momentum_right, "zero", axis=2, tiled=True)
    grad_local = jnp.transpose(
        lax.psum_scatter(
            jnp.einsum("esf,esd->fed", hidden, arrived, preferred_element_type=jnp.float32),
            "zero",
            scatter_dimension=0,
            tiled=True,
        ),
        (1, 0, 2),
    )
    merged = (
        MOMENTUM_DECAY * jnp.einsum("efr,erd->efd", momentum_left, right_full, precision=highest)
        + grad_local
    )
    sketched = jnp.einsum("efd,edr->efr", merged, sketch, precision=highest)
    basis = orthonormal(sketched)
    coeff_part = jnp.einsum("efr,efd->erd", basis, merged, precision=highest) / FF
    coefficients = lax.psum_scatter(coeff_part, "zero", scatter_dimension=2, tiled=True)
    return (basis, coefficients)


def solution(mesh):
    return jax.shard_map(
        body,
        mesh=mesh,
        in_specs=(
            P(("expert", "zero"), None),
            P(("expert", "zero"), None),
            P(("expert", "zero"), None),
            P("expert", "zero", None),
            P("expert", "zero", None),
            P("expert", None, "zero"),
            P("expert", None, None),
        ),
        out_specs=(P("expert", "zero", None), P("expert", None, "zero")),
        check_vma=False,
    )
```

profile of v0, /device:TPU:4, one launch (start us, length us, event | category | flops | bytes accessed | tf_op | source)
XLA Modules:
  0.0 433.0 jit_solution(7528596243765966278)
XLA Ops:
  7.2 0.0 copy-start
  7.2 0.0 copy-start.7
  7.2 0.0 reduce-scatter.3.cloned.1.call-start
  7.2 0.9 copy.26
  8.2 0.1 eq.29
  8.3 0.1 eq.25
  8.4 0.7 broadcast_multiply_fusion.1
  9.0 0.1 copy.28
  9.2 0.2 fusion.8
  9.4 0.0 copy-start.2
  9.4 0.8 copy-done.2
  10.2 1.1 broadcast_add_fusion
  11.3 0.9 copy.29
  12.1 0.1 copy.25
  12.2 0.1 mul.47
  12.3 2.2 convert_element_type.17
  14.6 0.0 copy-done.7
  14.6 0.1 copy.30
  14.7 0.1 mul.49
  14.8 1.4 fusion.7
  16.2 12.1 %scatter_custom_fusion = bf16[2048,2048]{1,0:T(8,128)(2,1)} fusion(s32[1024]{0:T(1024)S(1)} %bitcast.52, f32[128,2048]{1,0:T(8,128)} %convert_element_type.17, f32[1024]{0:T(1024)S(1)} %mul.49, bf16[]{:T(256)} %constant.54.clone.1), kind=kCustom, calls=%fused_computation.4 | custom fusion | flops 4194304 | bytes 9441282 | tf_op jit(solution)/shard_map/scatter | solution.py:38
  28.3 198.2 %all_to_all.18 = bf16[128,16,2048]{2,1,0:T(8,128)(2,1)} all-to-all(bf16[128,16,2048]{2,1,0:T(8,128)(2,1)} %bitcast.47), channel_id=1, replica_groups=mesh['expert'=64,'zero'=4] {'expert'}, dimensions={0} | all-to-all | bytes 16777216 | tf_op jit(solution)/shard_map/all_to_all | solution.py:41
  226.4 8.3 %copy.31 = bf16[2,64,16,2048]{3,2,1,0:T(8,128)(2,1)} copy(bf16[2,64,16,2048]{3,2,0,1:T(8,128)(2,1)} %bitcast.48) | data formatting | bytes 16777216 | tf_op jit(solution)/shard_map/all_to_all | solution.py:41
  234.7 0.0 copy-done
  234.7 12.6 %convolution_bitcast_fusion = f32[768,2,2048]{2,0,1:T(8,128)} fusion(bf16[2,1024,2048]{2,1,0:T(8,128)(2,1)} %bitcast.49, bf16[2,1024,768]{2,1,0:T(8,128)(2,1)S(1)} %copy-done), kind=kOutput, calls=%fused_computation.3 | convolution fusion | flops 6442450944 | bytes 24117248 | tf_op jit(solution)/shard_map/esf,esd->fed/dot_general | solution.py:45
  247.3 0.0 reduce-scatter.3.cloned.1.call-update
  247.3 0.0 reduce-scatter.5.cloned.1.call-start
  247.4 0.8 copy-done.5
  248.2 15.8 %all_gather.3 = f32[2,32,2048]{2,1,0:T(8,128)} all-gather(f32[2,32,512]{2,1,0:T(8,128)S(1)} %copy-done.5), channel_id=1, replica_groups=mesh['expert'=64,'zero'=4] {'zero'}, dimensions={2}, use_global_device_ids=true | all-gather | bytes 655360 | tf_op jit(solution)/shard_map/all_gather | solution.py:42
  264.0 98.7 %reduce-scatter.3.cloned.1.call-done = f32[192,2,2048]{2,0,1:T(8,128)} async-done(((f32[768,2,2048]{2,0,1:T(8,128)}), f32[192,2,2048]{2,0,1:T(8,128)}) %reduce-scatter.3.cloned.1.call-update) | async-done | bytes 3145744 | tf_op jit(solution)/shard_map/reduce_scatter | solution.py:44
  362.8 0.0 copy-done.6
  362.8 4.9 %bitcast_add_fusion = f32[2,192,2048]{2,1,0:T(8,128)S(1)} fusion(f32[192,2,2048]{2,0,1:T(8,128)} %reduce-scatter.3.cloned.1.call-done, f32[2,192,32]{1,2,0:T(8,128)S(1)} %copy-done.6, f32[2,32,2048]{2,1,0:T(8,128)} %all_gather.3), kind=kOutput, calls=%fused_computation.8 | convolution fusion | flops 303562752 | bytes 6864896 | tf_op jit(solution)/shard_map/efr,erd->efd/dot_general | solution.py:53
  367.7 1.7 copy-done.1
  369.4 0.0 copy-done.3
  369.4 3.1 fusion.14
  372.5 0.2 fusion.15
  372.7 15.0 %psum.7 = f32[2,32,32]{1,2,0:T(8,128)S(1)} all-reduce(f32[2,32,32]{1,2,0:T(8,128)S(1)} %fusion.15), channel_id=1, replica_groups=mesh['expert'=64,'zero'=4] {'zero'}, use_global_device_ids=true, to_apply=%region_5.6 | all-reduce | flops 2048 | bytes 16384 | tf_op jit(solution)/shard_map/psum | solution.py:21
  387.7 0.1 copy.35
  387.8 5.9 %custom-call.7 = f32[2,32,32]{2,1,0:T(8,128)S(1)} custom-call(f32[2,32,32]{2,1,0:T(8,128)S(1)} %fusion.13), custom_call_target="Cholesky" | custom-call | tf_op jit(solution)/shard_map/jit(cholesky)/cholesky | solution.py:22
  393.7 0.1 compare_reduce_fusion
  393.8 0.1 select_bitcast_fusion
  393.9 4.9 %custom-call.8 = f32[2,1,32,32]{2,3,1,0:T(8,128)S(1)} custom-call(f32[2,1,32,32]{3,2,1,0:T(8,128)S(1)} %select_bitcast_fusion), custom_call_target="InvertDiagBlocksLowerTriangular" | custom-call | tf_op jit(solution)/shard_map/triangular_solve | solution.py:23
  398.8 0.3 fusion.11
  399.1 0.0 copy-start.4
  399.1 4.7 %convolution_multiply_fusion = f32[2,32,2048]{2,1,0:T(8,128)} fusion(f32[2,32,192]{2,1,0:T(8,128)S(1)} %fusion.11, f32[2,192,2048]{2,1,0:T(8,128)} %copy-done.1), kind=kOutput, calls=%fused_computation.9 | convolution fusion | flops 302120960 | bytes 3719168 | tf_op jit(solution)/shard_map/efr,efd->erd/dot_general | solution.py:58
  403.8 0.0 reduce-scatter.5.cloned.1.call-update
  403.8 22.3 %reduce-scatter.5.cloned.1.call-done = f32[2,32,512]{2,1,0:T(8,128)} async-done(((f32[2,32,2048]{2,1,0:T(8,128)}), f32[2,32,512]{2,1,0:T(8,128)}) %reduce-scatter.5.cloned.1.call-update) | async-done | bytes 131088 | tf_op jit(solution)/shard_map/reduce_scatter | solution.py:59
  426.2 0.0 copy-done.4
  (13 shorter events, 0.1 us)
Async XLA Ops:
  7.2 227.6 %copy-start = (bf16[2,1024,768]{2,1,0:T(8,128)(2,1)S(1)}, bf16[2,1024,768]{2,1,0:T(8,128)(2,1)}, u32[]{:S(2)}) copy-start(bf16[2,1024,768]{2,1,0:T(8,128)(2,1)} %param.10) | copy-start | bytes 9437188
  7.2 7.4 %copy-start.7 = (f32[128,8]{0,1:T(8,128)S(1)}, f32[128,8]{0,1:T(8,128)}, u32[]{:S(2)}) copy-start(f32[128,8]{0,1:T(8,128)} %param.8) | copy-start | bytes 12292
  7.2 355.6 %reduce-scatter.3.cloned.1.call-start = ((), (), s32[]{:S(2)}) async-start(), calls=%async_computation.3 | async-start | bytes 15728640 | tf_op jit(solution)/shard_map/reduce_scatter | solution.py:44
  9.4 0.8 copy-start.2
  247.3 0.9 copy-start.5
  247.3 115.5 %copy-start.6 = (f32[2,192,32]{1,2,0:T(8,128)S(1)}, f32[2,192,32]{1,2,0:T(8,128)}, u32[]{:S(2)}) copy-start(f32[2,192,32]{1,2,0:T(8,128)} %param.11) | copy-start | bytes 147460
  247.3 178.9 %reduce-scatter.5.cloned.1.call-start = ((), (), s32[]{:S(2)}) async-start(), calls=%async_computation.4 | async-start | bytes 655360 | tf_op jit(solution)/shard_map/reduce_scatter | solution.py:59
  362.8 6.6 %copy-start.3 = (f32[2,2048,32]{1,2,0:T(8,128)S(1)}, f32[2,2048,32]{1,2,0:T(8,128)}, u32[]{:S(2)}) copy-start(f32[2,2048,32]{1,2,0:T(8,128)} %param.13) | copy-start | bytes 1572868
  367.7 1.7 copy-start.1
  399.1 27.1 %copy-start.4 = (f32[2,32,192]{2,1,0:T(8,128)}, f32[2,32,192]{2,1,0:T(8,128)S(1)}, u32[]{:S(2)}) copy-start(f32[2,32,192]{2,1,0:T(8,128)S(1)} %fusion.11) | copy-start | bytes 147460
Sparse Core Ops, SparseCore 0:
  247.4 115.2 reduce-scatter.2
  404.0 22.1 reduce-scatter.4
where the time goes:
time: 433 us
  blocking collectives  229 us (53%)
  waiting for transfers between devices  121 us (28%)
  other arithmetic  28.7 us (7%)
  matrix products  25.8 us (6%)
  between operations  14.2 us (3%)
  local copies, waits for them, and re-layouts  14.1 us (3%)
    all_to_all x1, blocking collectives, body(): lax.all_to_all(outgoing, 'expert', split_axis=0, concat_axis=1, tiled=True)  198 us
    reduce_scatter x1, waiting for transfers between devices, body(): lax.psum_scatter(jnp.einsum('esf,esd->fed', hidden, arrived, preferred_el...  98.7 us
    reduce_scatter x1, waiting for transfers between devices, body(): lax.psum_scatter(coeff_part, 'zero', scatter_dimension=2, tiled=True)  22.3 us
    all_gather x1, blocking collectives, body(): right_full = lax.all_gather(momentum_right, 'zero', axis=2, tiled=True)  15.8 us
    psum x1, blocking collectives, orthonormal(): gram = lax.psum(local_gram, 'zero') / FF  15 us
    dot_general x1, matrix products, body(): jnp.einsum('esf,esd->fed', hidden, arrived, preferred_element_type=jnp.fl...  12.6 us
    scatter x1, other arithmetic, body(): jnp.zeros((experts * CAP, width), jnp.bfloat16).at[target]  12.1 us
  transfers between devices with their start and end apart: 2, of which 2 were waited for; matrix products, arithmetic and copies ran while one was open for 0% of the time, Pallas kernels for 0%

commit v1 on v0

--- a/solution.py
+++ b/solution.py
@@ -6,6 +6,18 @@
 FF = 768
 CAP = 16
 MOMENTUM_DECAY = 0.9
+
+
+def collect(x, axis, dim):
+    ways, here, step = (lax.axis_size(axis), lax.axis_index(axis), x.shape[dim])
+    line, have = (x, 1)
+    while have < ways:
+        line = jnp.concatenate(
+            [line, lax.ppermute(line, axis, [(d, (d - have) % ways) for d in range(ways)])],
+            axis=dim,
+        )
+        have = 2 * have
+    return jnp.roll(line, here * step, axis=dim)
 
 
 def slot_table(ids_block, count):
@@ -39,7 +51,7 @@
     )
     outgoing = outgoing.reshape(experts, CAP, width)
     arrived = lax.all_to_all(outgoing, "expert", split_axis=0, concat_axis=1, tiled=True)
-    right_full = lax.all_gather(momentum_right, "zero", axis=2, tiled=True)
+    right_full = collect(momentum_right, "zero", 2)
     grad_local = jnp.transpose(
         lax.psum_scatter(
             jnp.einsum("esf,esd->fed", hidden, arrived, preferred_element_type=jnp.float32),

time: 433 us -> 437 us (level)
  blocking collectives: 229 us -> 214 us
  local copies, waits for them, and re-layouts: 14.1 us -> 20.1 us
  waiting for transfers between devices: 121 us -> 127 us
  starting transfers between devices: 0.08 us -> 5.72 us
    all_gather x1 -> x0, blocking collectives: 15.8 us -> none  [body(): right_full = lax.all_gather(momentum_right, 'zero', axis=2, tiled=True)]
    ppermute x0 -> x2, waiting for transfers between devices: none -> 12.7 us  [collect(): lax.ppermute(line, axis, [(d, (d - have) % ways) for d in range(ways)])]
    reduce_scatter x1, waiting for transfers between devices: 98.7 us -> 92.1 us  [body(): lax.psum_scatter(jnp.einsum('esf,esd->fed', hidden, arrived, preferred_el...]
    ppermute x0 -> x2, starting transfers between devices: none -> 5.64 us  [collect(): lax.ppermute(line, axis, [(d, (d - have) % ways) for d in range(ways)])]
  transfers between devices with their start and end apart: 2 -> 4, of which waited for: 2 -> 4; matrix products, arithmetic and copies ran while one was open for 0% -> 2% of each run, Pallas kernels for 0% -> 0%
where the time goes in v1:
time: 437 us
  blocking collectives  214 us (49%)
  waiting for transfers between devices  127 us (29%)
  other arithmetic  29.6 us (7%)
  matrix products  25.8 us (6%)
  local copies, waits for them, and re-layouts  20.1 us (5%)
  between operations  14.2 us (3%)
  starting transfers between devices  5.72 us (1%)
    all_to_all x1, blocking collectives, body(): lax.all_to_all(outgoing, 'expert', split_axis=0, concat_axis=1, tiled=True)  198 us
    reduce_scatter x1, waiting for transfers between devices, body(): lax.psum_scatter(jnp.einsum('esf,esd->fed', hidden, arrived, preferred_el...  92.1 us
    reduce_scatter x1, waiting for transfers between devices, body(): lax.psum_scatter(coeff_part, 'zero', scatter_dimension=2, tiled=True)  22.4 us
    psum x1, blocking collectives, orthonormal(): gram = lax.psum(local_gram, 'zero') / FF  15.9 us
    ppermute x2, waiting for transfers between devices, collect(): lax.ppermute(line, axis, [(d, (d - have) % ways) for d in range(ways)])  12.7 us
    dot_general x1, matrix products, body(): jnp.einsum('esf,esd->fed', hidden, arrived, preferred_element_type=jnp.fl...  12.6 us
    scatter x1, other arithmetic, body(): jnp.zeros((experts * CAP, width), jnp.bfloat16).at[target]  12.1 us
  transfers between devices with their start and end apart: 4, of which 4 were waited for; matrix products, arithmetic and copies ran while one was open for 2% of the time, Pallas kernels for 0%

profile of v1, /device:TPU:4, one launch (start us, length us, event | category | flops | bytes accessed | tf_op | source)
XLA Modules:
  0.0 436.6 jit_solution(295096192944677044)
XLA Ops:
  7.2 0.0 reduce-scatter.3.cloned.1.call-start
  7.2 0.8 broadcast_multiply_fusion.1
  8.1 0.9 copy.26
  8.9 0.1 eq.32
  9.0 0.1 eq.28
  9.1 0.1 copy.25
  9.2 0.1 mul.55
  9.3 0.1 copy.28
  9.4 0.2 fusion.8
  9.6 0.8 copy-done.2
  10.5 1.1 broadcast_add_fusion
  11.5 0.9 copy.29
  12.4 2.2 convert_element_type.17
  14.6 0.1 copy.30
  14.7 0.1 mul.57
  14.8 1.4 fusion.7
  16.3 12.1 %scatter_custom_fusion = bf16[2048,2048]{1,0:T(8,128)(2,1)} fusion(s32[1024]{0:T(1024)S(1)} %bitcast.53, f32[128,2048]{1,0:T(8,128)} %convert_element_type.17, f32[1024]{0:T(1024)S(1)} %mul.57, bf16[]{:T(256)} %constant.82.clone.1), kind=kCustom, calls=%fused_computation.4 | custom fusion | flops 4194304 | bytes 9441282 | tf_op jit(solution)/shard_map/scatter | solution.py:50
  28.3 198.2 %all_to_all.18 = bf16[128,16,2048]{2,1,0:T(8,128)(2,1)} all-to-all(bf16[128,16,2048]{2,1,0:T(8,128)(2,1)} %bitcast.48), channel_id=1, replica_groups=mesh['expert'=64,'zero'=4] {'expert'}, dimensions={0} | all-to-all | bytes 16777216 | tf_op jit(solution)/shard_map/all_to_all | solution.py:53
  226.5 8.3 %copy.31 = bf16[2,64,16,2048]{3,2,1,0:T(8,128)(2,1)} copy(bf16[2,64,16,2048]{3,2,0,1:T(8,128)(2,1)} %bitcast.49) | data formatting | bytes 16777216 | tf_op jit(solution)/shard_map/all_to_all | solution.py:53
  234.8 12.6 %convolution_bitcast_fusion = f32[768,2,2048]{2,0,1:T(8,128)} fusion(bf16[2,1024,2048]{2,1,0:T(8,128)(2,1)} %bitcast.50, bf16[2,1024,768]{2,1,0:T(8,128)(2,1)S(1)} %copy-done), kind=kOutput, calls=%fused_computation.3 | convolution fusion | flops 6442450944 | bytes 24117248 | tf_op jit(solution)/shard_map/esf,esd->fed/dot_general | solution.py:57
  247.4 0.0 reduce-scatter.3.cloned.1.call-update
  247.4 0.0 reduce-scatter.5.cloned.1.call-start
  247.4 0.8 copy-done.3
  248.3 3.0 collective-permute-start
  251.3 2.5 collective-permute-done
  253.8 0.7 pad_maximum_fusion
  254.5 2.6 collective-permute-start.1
  257.1 0.7 constant_dynamic-update-slice_fusion.5
  257.8 0.7 constant_dynamic-update-slice_fusion.4
  258.5 10.2 %collective-permute-done.1 = f32[2,32,1024]{2,1,0:T(8,128)} collective-permute-done((f32[2,32,1024]{2,1,0:T(8,128)}, f32[2,32,1024]{2,1,0:T(8,128)}, u32[]{:S(2)}, u32[]{:S(2)}) %collective-permute-start.1) | collective-permute-done | bytes 262176 | tf_op jit(solution)/shard_map/ppermute | solution.py:16
  268.7 1.7 constant_dynamic-update-slice_fusion.3
  270.4 0.7 constant_dynamic-update-slice_fusion.2
  271.0 0.7 constant_dynamic-update-slice_fusion.1
  271.7 1.7 constant_dynamic-update-slice_fusion
  273.4 92.1 %reduce-scatter.3.cloned.1.call-done = f32[192,2,2048]{2,0,1:T(8,128)} async-done(((f32[768,2,2048]{2,0,1:T(8,128)}), f32[192,2,2048]{2,0,1:T(8,128)}) %reduce-scatter.3.cloned.1.call-update) | async-done | bytes 3145744 | tf_op jit(solution)/shard_map/reduce_scatter | solution.py:56
  365.5 4.9 %bitcast_add_fusion = f32[2,192,2048]{2,1,0:T(8,128)S(1)} fusion(f32[192,2,2048]{2,0,1:T(8,128)} %reduce-scatter.3.cloned.1.call-done, f32[2,192,32]{1,2,0:T(8,128)S(1)} %copy-done.6, f32[2,32,4096]{2,1,0:T(8,128)} %constant_dynamic-update-slice_fusion, s32[]{:T(128)S(6)} %select_n.28), kind=kOutput, calls=%fused_computation.8 | convolution fusion | flops 303562752 | bytes 6864900 | tf_op jit(solution)/shard_map/efr,erd->efd/dot_general | solution.py:65
  370.4 1.7 copy-done.1
  372.1 3.1 fusion.16
  375.2 0.2 fusion.17
  375.4 15.9 %psum.7 = f32[2,32,32]{1,2,0:T(8,128)S(1)} all-reduce(f32[2,32,32]{1,2,0:T(8,128)S(1)} %fusion.17), channel_id=1, replica_groups=mesh['expert'=64,'zero'=4] {'zero'}, use_global_device_ids=true, to_apply=%region_5.6 | all-reduce | flops 2048 | bytes 16384 | tf_op jit(solution)/shard_map/psum | solution.py:33
  391.3 0.1 copy.35
  391.4 5.9 %custom-call.7 = f32[2,32,32]{2,1,0:T(8,128)S(1)} custom-call(f32[2,32,32]{2,1,0:T(8,128)S(1)} %fusion.14), custom_call_target="Cholesky" | custom-call | tf_op jit(solution)/shard_map/jit(cholesky)/cholesky | solution.py:34
  397.3 0.1 compare_reduce_fusion
  397.4 0.1 select_bitcast_fusion
  397.5 4.9 %custom-call.8 = f32[2,1,32,32]{2,3,1,0:T(8,128)S(1)} custom-call(f32[2,1,32,32]{3,2,1,0:T(8,128)S(1)} %select_bitcast_fusion), custom_call_target="InvertDiagBlocksLowerTriangular" | custom-call | tf_op jit(solution)/shard_map/triangular_solve | solution.py:35
  402.4 0.3 fusion.12
  402.7 4.7 %convolution_multiply_fusion = f32[2,32,2048]{2,1,0:T(8,128)} fusion(f32[2,32,192]{2,1,0:T(8,128)S(1)} %fusion.12, f32[2,192,2048]{2,1,0:T(8,128)} %copy-done.1), kind=kOutput, calls=%fused_computation.9 | convolution fusion | flops 302120960 | bytes 3719168 | tf_op jit(solution)/shard_map/efr,efd->erd/dot_general | solution.py:70
  407.4 22.4 %reduce-scatter.5.cloned.1.call-done = f32[2,32,512]{2,1,0:T(8,128)} async-done(((f32[2,32,2048]{2,1,0:T(8,128)}), f32[2,32,512]{2,1,0:T(8,128)}) %reduce-scatter.5.cloned.1.call-update) | async-done | bytes 131088 | tf_op jit(solution)/shard_map/reduce_scatter | solution.py:71
  (23 shorter events, 0.2 us)
Async XLA Ops:
  7.2 227.6 %copy-start = (bf16[2,1024,768]{2,1,0:T(8,128)(2,1)S(1)}, bf16[2,1024,768]{2,1,0:T(8,128)(2,1)}, u32[]{:S(2)}) copy-start(bf16[2,1024,768]{2,1,0:T(8,128)(2,1)} %param.10) | copy-start | bytes 9437188
  7.2 7.5 %copy-start.7 = (f32[128,8]{0,1:T(8,128)S(1)}, f32[128,8]{0,1:T(8,128)}, u32[]{:S(2)}) copy-start(f32[128,8]{0,1:T(8,128)} %param.8) | copy-start | bytes 12292
  7.2 358.3 %reduce-scatter.3.cloned.1.call-start = ((), (), s32[]{:S(2)}) async-start(), calls=%async_computation.3 | async-start | bytes 15728640 | tf_op jit(solution)/shard_map/reduce_scatter | solution.py:56
  9.6 0.8 copy-start.2
  247.4 0.9 copy-start.3
  247.4 118.1 %copy-start.6 = (f32[2,192,32]{1,2,0:T(8,128)S(1)}, f32[2,192,32]{1,2,0:T(8,128)}, u32[]{:S(2)}) copy-start(f32[2,192,32]{1,2,0:T(8,128)} %param.11) | copy-start | bytes 147460
  247.4 182.4 %reduce-scatter.5.cloned.1.call-start = ((), (), s32[]{:S(2)}) async-start(), calls=%async_computation.4 | async-start | bytes 655360 | tf_op jit(solution)/shard_map/reduce_scatter | solution.py:71
  248.3 5.5 %collective-permute-start = (f32[2,32,512]{2,1,0:T(8,128)S(1)}, f32[2,32,512]{2,1,0:T(8,128)S(1)}, u32[]{:S(2)}, u32[]{:S(2)}) collective-permute-start(f32[2,32,512]{2,1,0:T(8,128)S(1)} %copy-done.3), channel_id=1, source_target_pairs={{0,3},{1,0},{2,1},{3,2},{4,7},{5,4},{6,5},{7,6},{8,11},{9,8},{10,9... | collective-permute-start | bytes 393224 | tf_op jit(solution)/shard_map/ppermute | solution.py:16
  254.5 14.2 %collective-permute-start.1 = (f32[2,32,1024]{2,1,0:T(8,128)}, f32[2,32,1024]{2,1,0:T(8,128)}, u32[]{:S(2)}, u32[]{:S(2)}) collective-permute-start(f32[2,32,1024]{2,1,0:T(8,128)} %pad_maximum_fusion), channel_id=1, source_target_pairs={{0,2},{1,3},{2,0},{3,1},{4,6},{5,7},{6,4},{7,5},{8,10},{9,11},{10,... | collective-permute-start | bytes 786440 | tf_op jit(solution)/shard_map/ppermute | solution.py:16
  365.5 6.6 %copy-start.4 = (f32[2,2048,32]{1,2,0:T(8,128)S(1)}, f32[2,2048,32]{1,2,0:T(8,128)}, u32[]{:S(2)}) copy-start(f32[2,2048,32]{1,2,0:T(8,128)} %param.13) | copy-start | bytes 1572868
  370.4 1.7 copy-start.1
  402.7 27.1 %copy-start.5 = (f32[2,32,192]{2,1,0:T(8,128)}, f32[2,32,192]{2,1,0:T(8,128)S(1)}, u32[]{:S(2)}) copy-start(f32[2,32,192]{2,1,0:T(8,128)S(1)} %fusion.12) | copy-start | bytes 147460
Sparse Core Ops, SparseCore 0:
  247.5 117.9 reduce-scatter.2
  407.5 22.1 reduce-scatter.4
